TPU v7x, 256 devices: a whole 4x4x8 slice. The times are simulated.
256 devices in a mesh: rows: 128 (over x, z, y_lo, core), cols: 2 (over y_hi).
Axes of the slice: x: 4, y: 4 (y_hi: 2, y_lo: 2; y = y_hi * 2 + y_lo), z: 8, core: 2. Of those that a mesh axis runs over, the one named last changes fastest.
Arguments:
- latent: bfloat16 [4, 3072, 48], P(None, 'rows', 'cols'), may hold values from -6 to 6
- offsets: int32 [2], replicated, may hold values from 0 to 23, as said below
- timestep: int32 [1], replicated, may hold values from 0 to 999
- conv_in_weight: bfloat16 [3, 3, 4, 320], replicated, may hold values from -1 to 1
- conv_in_bias: float32 [320], replicated, may hold values from -3 to 3
- norm_one_gain: float32 [320], replicated, may hold values from 0.1 to 1.9
- norm_one_shift: float32 [320], replicated, may hold values from -3 to 3
- conv_one_weight: bfloat16 [3, 3, 320, 320], replicated, may hold values from -0.109375 to 0.109375
- conv_one_bias: float32 [320], replicated, may hold values from -4 to 4
- time_one_weight: bfloat16 [320, 1280], replicated, may hold values from -0.3125 to 0.3125
- time_one_bias: float32 [1280], replicated, may hold values from -3 to 3
- time_two_weight: bfloat16 [1280, 1280], replicated, may hold values from -0.15625 to 0.15625
- time_two_bias: float32 [1280], replicated, may hold values from -3 to 3
- time_proj_weight: bfloat16 [1280, 320], replicated, may hold values from -0.15625 to 0.15625
- time_proj_bias: float32 [320], replicated, may hold values from -4 to 4
- norm_two_gain: float32 [320], replicated, may hold values from 0.1 to 1.9
- norm_two_shift: float32 [320], replicated, may hold values from -3 to 3
- conv_two_weight: bfloat16 [3, 3, 320, 320], replicated, may hold values from -0.109375 to 0.109375
- conv_two_bias: float32 [320], replicated, may hold values from -3 to 3
Outputs:
- blended: float32 [3072, 48, 320], P('rows', 'cols')
Inputs may be any that keep to these rules, and one draw needn't show every extreme that they name: The two offsets differ; one of them equals 23.
All inputs are finite; a program needn't handle non-finite values.
Results may differ from a plain program's by a relative error of at most 0.0028.
Values may be sent and summed in bfloat16 or wider, within the bound.
A program may use at most 64 MiB of HBM per device.

v0:
```python
import math

import jax
import jax.numpy as jnp
from jax import lax
from jax.sharding import PartitionSpec as P

C = 320
LATC = 4
GROUPS = 32
STRIDE = 24
TAIL = 8
WIN = 32


def from_behind(value, axis, steps):
    count = lax.axis_size(axis)
    pairs = [(source, (source + steps) % count) for source in range(count)]
    return lax.ppermute(value, axis, pairs)


def time_vector(
    timestep,
    time_one_weight,
    time_one_bias,
    time_two_weight,
    time_two_bias,
    time_proj_weight,
    time_proj_bias,
):
    half = C // 2
    freqs = jnp.exp(-math.log(10000.0) * jnp.arange(half).astype(jnp.float32) / half)
    angles = timestep.astype(jnp.float32)[0] * freqs
    sinus = jnp.concatenate([jnp.cos(angles), jnp.sin(angles)])[None].astype(jnp.bfloat16)
    embed_one = jax.nn.silu(
        jnp.dot(sinus, time_one_weight, preferred_element_type=jnp.float32) + time_one_bias
    ).astype(jnp.bfloat16)
    embed_two = jax.nn.silu(
        jnp.dot(embed_one, time_two_weight, preferred_element_type=jnp.float32) + time_two_bias
    ).astype(jnp.bfloat16)
    return (
        jnp.dot(embed_two, time_proj_weight, preferred_element_type=jnp.float32)[0] + time_proj_bias
    )


def convolve(image, kernel):
    return lax.conv_general_dilated(
        image,
        kernel,
        (1, 1),
        "SAME",
        dimension_numbers=("NHWC", "HWIO", "NHWC"),
        preferred_element_type=jnp.float32,
    )


def group_norm(values, gain, shift):
    batch, height, width, chans = values.shape
    grouped = values.reshape(batch, height, width, GROUPS, chans // GROUPS)
    mean = jnp.mean(grouped, axis=(1, 2, 4), keepdims=True)
    var = jnp.mean((grouped - mean) ** 2, axis=(1, 2, 4), keepdims=True)
    normed = ((grouped - mean) / jnp.sqrt(var + 1e-05)).reshape(batch, height, width, chans)
    return normed * gain + shift


def combine_rows(canvas):
    own = canvas[:STRIDE]
    middle = canvas[STRIDE : 2 * STRIDE]
    tail = canvas[2 * STRIDE :]
    near = from_behind(middle, "rows", 1)
    far = from_behind(tail.astype(jnp.bfloat16), "rows", 2).astype(tail.dtype)
    return (own + near).at[:TAIL].add(far)


def combine_cols(canvas):
    own = canvas[:, :STRIDE]
    near = from_behind(canvas[:, STRIDE : 2 * STRIDE], "cols", 1)
    return (own + near).at[:, :TAIL].add(canvas[:, 2 * STRIDE :])


def on_device(
    latent,
    offsets,
    timestep,
    conv_in_weight,
    conv_in_bias,
    norm_one_gain,
    norm_one_shift,
    conv_one_weight,
    conv_one_bias,
    time_one_weight,
    time_one_bias,
    time_two_weight,
    time_two_bias,
    time_proj_weight,
    time_proj_bias,
    norm_two_gain,
    norm_two_shift,
    conv_two_weight,
    conv_two_bias,
):
    row_off = offsets[0]
    col_off = offsets[1]
    below = from_behind(latent, "rows", -1)
    further = from_behind(latent[:, :TAIL], "rows", -2)
    tall = jnp.concatenate([latent, below, further], 1)
    right = from_behind(tall, "cols", -1)
    extended = jnp.concatenate([tall, right, tall[:, :, :TAIL]], 2)
    anchor = jnp.zeros((), jnp.int32)
    window = lax.dynamic_slice(extended, (anchor, row_off, col_off), (LATC, WIN, WIN))
    window = jnp.transpose(window, (1, 2, 0))[None]
    time_shift = time_vector(
        timestep,
        time_one_weight,
        time_one_bias,
        time_two_weight,
        time_two_bias,
        time_proj_weight,
        time_proj_bias,
    )
    start = (convolve(window, conv_in_weight) + conv_in_bias).astype(jnp.bfloat16)
    act_one = jax.nn.silu(
        group_norm(start.astype(jnp.float32), norm_one_gain, norm_one_shift)
    ).astype(jnp.bfloat16)
    inner = convolve(act_one, conv_one_weight) + conv_one_bias + time_shift
    act_two = jax.nn.silu(group_norm(inner, norm_two_gain, norm_two_shift)).astype(jnp.bfloat16)
    window_out = (convolve(act_two, conv_two_weight) + conv_two_bias + start.astype(jnp.float32))[0]
    side = STRIDE + WIN
    canvas = lax.dynamic_update_slice(
        jnp.zeros((side, side, C), jnp.float32), window_out, (row_off, col_off, anchor)
    )
    total = combine_cols(combine_rows(canvas))
    positions = jnp.arange(STRIDE)
    row_count = 1.0 + ((positions - row_off) % STRIDE < TAIL).astype(jnp.float32)
    col_count = 1.0 + ((positions - col_off) % STRIDE < TAIL).astype(jnp.float32)
    return total / (row_count[:, None] * col_count[None, :])[:, :, None]


def solution(mesh):
    return jax.shard_map(
        on_device,
        mesh=mesh,
        in_specs=(
            P(None, "rows", "cols"),
            P(),
            P(),
            P(),
            P(),
            P(),
            P(),
            P(),
            P(),
            P(),
            P(),
            P(),
            P(),
            P(),
            P(),
            P(),
            P(),
            P(),
            P(),
        ),
        out_specs=P("rows", "cols", None),
        check_vma=False,
    )
```

profile of v0, /device:TPU:1, one launch (start us, length us, event | category | flops | bytes accessed | tf_op | source)
XLA Modules:
  0.0 121.9 jit_solution(14488620368075541862)
XLA Ops:
  0.0 1.0 copy.36
  1.0 3.3 %collective-permute-start = (bf16[4,24,24]{1,2,0:T(8,128)(2,1)S(1)}, bf16[4,24,24]{1,2,0:T(8,128)(2,1)S(1)}, u32[]{:S(2)}, u32[]{:S(2)}) collective-permute-start(bf16[4,24,24]{1,2,0:T(8,128)(2,1)S(1)} %copy.36), channel_id=1, source_target_pairs={{0,254},{2,0},{4,2},{6,4},{8,6},{10,8},{12,10},{14,12},{16,14},{18... | collective-permute-start | bytes 13832 | tf_op jit(solution)/shard_map/ppermute | solution.py:19
  4.3 7.1 %collective-permute-start.1 = (bf16[4,8,24]{1,2,0:T(8,128)(2,1)S(1)}, bf16[4,8,24]{1,2,0:T(8,128)(2,1)S(1)}, u32[]{:S(2)}, u32[]{:S(2)}) collective-permute-start(bf16[4,8,24]{1,2,0:T(8,128)(2,1)S(1)} %bitcast.39), channel_id=1, source_target_pairs={{0,252},{2,254},{4,0},{6,2},{8,4},{10,6},{12,8},{14,10},{16,12},{1... | collective-permute-start | bytes 4616 | tf_op jit(solution)/shard_map/ppermute | solution.py:19
  12.1 0.1 pad_maximum_fusion.1
  12.2 1.5 %convolution_reduce_fusion.1 = f32[1280]{0:T(1024)S(1)} fusion(bf16[320,1]{0,1:T(2,128)(2,1)S(1)} %reshape.286, bf16[320,1280]{1,0:T(8,128)(2,1)} %param.32), kind=kOutput, calls=%fused_computation.42 | convolution fusion | flops 819200 | bytes 824960 | tf_op jit(solution)/shard_map/dot_general | solution.py:36
  13.6 0.7 multiply_convert_fusion.3
  14.4 0.0 copy-start.8
  14.4 0.0 copy-start.3
  14.4 0.0 copy-start.15
  14.4 0.5 convolution_reduce_fusion
  15.0 0.3 convolution_reduce_fusion.2
  15.4 0.1 pad_maximum_fusion
  15.5 2.9 %collective-permute-start.2 = (bf16[4,56,24]{1,2,0:T(8,128)(2,1)S(1)}, bf16[4,56,24]{1,2,0:T(8,128)(2,1)S(1)}, u32[]{:S(2)}, u32[]{:S(2)}) collective-permute-start(bf16[4,56,24]{1,2,0:T(8,128)(2,1)S(1)} %pad_maximum_fusion), channel_id=1, source_target_pairs={{0,1},{1,0},{2,3},{3,2},{4,5},{5,4},{6,7},{7,6},{8,9},{9,8},{10,11... | collective-permute-start | bytes 32264 | tf_op jit(solution)/shard_map/ppermute | solution.py:19
  18.3 0.6 fusion.66
  22.8 0.2 fusion.50
  23.0 0.2 copy.39
  23.2 0.1 slice.99
  23.3 0.0 copy-start.6
  23.3 2.1 %fusion.10 = (f32[320]{0:T(512)S(1)}, bf16[32,8,5,320]{3,1,2,0:T(8,128)(2,1)}) fusion(pred[8,5]{0,1:T(8,128)(4,1)S(1)} %copy-done.3, f32[320]{0:T(512)S(1)} %copy-done.15, bf16[3,3,4,320]{3,2,1,0:T(4,128)(2,1)S(1)} %copy-done.14, bf16[32,1,7,2,4]{2,4,3,0,1:T(4,128)(2,1)S(1)} %slice.99, bf16[32,1,8,5,4]{2,4,3,0,1:T(4,128)(2,1)S(1)} %copy.39), kind=kOutput, calls=%fused_computation.16 | convolution fusion | flops 31377088 | bytes 858664 | tf_op jit(solution)/shard_map/conv_general_dilated | solution.py:47
  25.5 0.1 reduce_sum.47
  25.6 0.1 reduce_sum.51
  25.7 0.1 sub.64
  25.8 0.1 sub.65
  25.9 1.6 %fusion.7 = f32[320]{0:T(512)S(1)} fusion(bf16[32,8,5,320]{3,1,2,0:T(8,128)(2,1)} %get-tuple-element.36, f32[320]{0:T(512)S(1)} %sub.65, pred[8,5]{0,1:T(8,128)(4,1)S(1)} %copy-done.3), kind=kLoop, calls=%fused_computation.13 | loop fusion | flops 2047680 | bytes 821800 | tf_op jit(solution)/shard_map/reduce_sum | solution.py:61
  27.5 0.1 reduce_sum.53
  27.6 0.1 reduce_sum.54
  27.8 0.1 div.80
  27.8 0.1 div.81
  28.0 2.1 %fusion.33 = bf16[32,1,8,5,320]{4,2,3,0,1:T(8,128)(2,1)S(1)} fusion(bf16[32,8,5,320]{3,1,2,0:T(8,128)(2,1)} %get-tuple-element.36, f32[320]{0:T(512)S(1)} %copy-done.6, f32[320]{0:T(512)S(1)} %copy-done.7, f32[320]{0:T(512)S(1)} %div.81, f32[320]{0:T(512)S(1)} %sub.65, pred[8,5]{0,1:T(8,128)(4,1)S(1)} %copy-done.3), kind=kLoop, calls=%fused_computation.45 | loop fusion | flops 4505600 | bytes 1643560 | tf_op jit(solution)/shard_map/convert_element_type | solution.py:124
  30.1 0.1 fusion.65
  30.2 5.5 %select_reduce_fusion.1 = (f32[320]{0:T(512)S(1)}, f32[32,8,5,320]{3,1,2,0:T(8,128)}) fusion(f32[320]{0:T(512)S(1)} %add.176, f32[320]{0:T(512)S(1)} %copy-done.5, pred[8,5]{0,1:T(8,128)(4,1)S(1)} %copy-done.3, bf16[3,3,320,320]{3,2,1,0:T(8,128)(2,1)S(1)} %copy-done.12, bf16[32,1,7,1,320]{4,2,3,0,1:T(8,128)(2,1)S(1)} %get-tuple-element.32, ...), kind=kOutput, calls=%fused_computation.19 | convolution fusion | flops 2317516544 | bytes 4591400 | tf_op jit(solution)/shard_map/conv_general_dilated | solution.py:47
  35.7 0.1 reduce_sum.59
  35.8 0.1 reduce_sum.72
  35.9 0.1 sub.68
  36.0 0.1 sub.69
  36.1 2.0 %select_reduce_fusion = f32[320]{0:T(512)S(1)} fusion(f32[32,8,5,320]{3,1,2,0:T(8,128)} %get-tuple-element.38, f32[320]{0:T(512)S(1)} %sub.69, f32[320]{0:T(512)S(1)} %add.176, f32[320]{0:T(512)S(1)} %copy-done.5, pred[8,5]{0,1:T(8,128)(4,1)S(1)} %copy-done.3), kind=kLoop, calls=%fused_computation.18 | loop fusion | flops 2457280 | bytes 1643560 | tf_op jit(solution)/shard_map/reduce_sum | solution.py:61
  38.1 0.1 reduce_sum.74
  38.3 0.1 reduce_sum.75
  38.4 0.1 div.91
  38.5 0.1 div.92
  38.6 2.5 %select_bitcast_fusion = bf16[32,1,8,5,320]{4,2,3,0,1:T(8,128)(2,1)S(1)} fusion(f32[320]{0:T(512)S(1)} %copy-done.10, f32[320]{0:T(512)S(1)} %copy-done.11, f32[320]{0:T(512)S(1)} %div.92, f32[320]{0:T(512)S(1)} %sub.69, f32[320]{0:T(512)S(1)} %add.176, f32[32,8,5,320]{3,1,2,0:T(8,128)} %get-tuple-element.38, f32[320]{0:T(512)S(1)} %copy-done.5, ...), kind=kLoop, calls=%fused_computation.46 | loop fusion | flops 4915200 | bytes 2465320 | tf_op jit(solution)/shard_map/convert_element_type | solution.py:126
  41.1 0.1 fusion.64
  41.2 4.5 %convert_add_fusion = f32[32,8,5,320]{3,1,2,0:T(8,128)S(1)} fusion(bf16[32,8,5,320]{3,1,2,0:T(8,128)(2,1)S(1)} %copy-done.1, bf16[3,3,320,320]{3,2,1,0:T(8,128)(2,1)S(1)} %copy-done.13, bf16[32,1,7,1,320]{4,2,3,0,1:T(8,128)(2,1)S(1)} %get-tuple-element.30, bf16[32,1,7,1,320]{4,2,3,0,1:T(8,128)(2,1)S(1)} %get-tuple-element.29, ...), kind=kOutput, calls=%fused_computation | convolution fusion | flops 2317107200 | bytes 5408000 | tf_op jit(solution)/shard_map/conv_general_dilated | solution.py:47
  45.8 0.4 copy.40
  46.2 0.1 slice_bitcast_fusion
  46.3 2.1 %copy.41 = f32[32,32,320]{2,1,0:T(8,128)} copy(f32[32,32,320]{2,0,1:T(8,128)S(1)} %slice_bitcast_fusion) | data formatting | bytes 2621440 | tf_op jit(solution)/shard_map/squeeze | solution.py:127
  48.4 2.5 %broadcast_in_dim.4 = f32[56,56,320]{2,1,0:T(8,128)} broadcast(f32[]{:T(128)} %constant.86.clone.1), dimensions={} | broadcast | bytes 4014084 | tf_op jit(solution)/shard_map/broadcast_in_dim | solution.py:130
  50.8 8.8 %dynamic_update_slice.3 = f32[56,56,320]{2,1,0:T(8,128)} dynamic-update-slice(f32[56,56,320]{2,1,0:T(8,128)} %broadcast_in_dim.4, f32[32,32,320]{2,1,0:T(8,128)} %copy.41, s32[]{:T(128)S(6)} %select_n.27, s32[]{:T(128)S(6)} %select_n.28, s32[]{:T(128)} %constant.87.clone.1) | dynamic-update-slice | bytes 2621444 | tf_op jit(solution)/shard_map/dynamic_update_slice | solution.py:129
  59.6 1.7 %slice.106 = f32[24,56,320]{2,1,0:T(8,128)S(1)} slice(f32[56,56,320]{2,1,0:T(8,128)} %dynamic_update_slice.3), slice={[24:48], [0:56], [0:320]} | slice | bytes 3440640 | tf_op jit(solution)/shard_map/slice | solution.py:68
  61.3 1.1 collective-permute-start.3
  62.4 1.1 slice.124
  63.6 0.1 collective-permute-start.4
  63.7 25.1 %collective-permute-done.3 = f32[24,56,320]{2,1,0:T(8,128)S(1)} collective-permute-done((f32[24,56,320]{2,1,0:T(8,128)S(1)}, f32[24,56,320]{2,1,0:T(8,128)S(1)}, u32[]{:S(2)}, u32[]{:S(2)}) %collective-permute-start.3) | collective-permute-done | bytes 1720352 | tf_op jit(solution)/shard_map/ppermute | solution.py:19
  88.7 1.8 %slice_add_fusion = f32[24,56,320]{2,1,0:T(8,128)S(1)} fusion(f32[24,56,320]{2,1,0:T(8,128)S(1)} %collective-permute-done.3, f32[56,56,320]{2,1,0:T(8,128)} %dynamic_update_slice.3), kind=kLoop, calls=%fused_computation.11 | loop fusion | flops 430080 | bytes 5160960 | tf_op jit(solution)/shard_map/add | solution.py:72
  90.6 7.7 %collective-permute-done.4 = bf16[8,56,320]{2,1,0:T(8,128)(2,1)S(1)} collective-permute-done((bf16[8,56,320]{2,1,0:T(8,128)(2,1)S(1)}, bf16[8,56,320]{2,1,0:T(8,128)(2,1)S(1)}, u32[]{:S(2)}, u32[]{:S(2)}) %collective-permute-start.4) | collective-permute-done | bytes 286752 | tf_op jit(solution)/shard_map/ppermute | solution.py:19
  98.3 0.1 fusion.34
  98.4 0.1 slice.110
  98.5 0.6 collective-permute-start.5
  99.1 1.3 %fusion.51 = (f32[24]{0:T(128)S(1)}, f32[24]{0:T(128)S(1)}) fusion(s32[]{:T(128)} %bitcast, s32[]{:T(128)} %bitcast.1), kind=kLoop, calls=%fused_computation.86 | loop fusion | flops 480 | bytes 200 | tf_op jit(solution)/shard_map/add | solution.py:134
  100.4 0.1 broadcast_multiply_fusion
  100.4 20.2 %collective-permute-done.5 = f32[24,24,320]{2,1,0:T(8,128)S(1)} collective-permute-done((f32[24,24,320]{2,1,0:T(8,128)S(1)}, f32[24,24,320]{2,1,0:T(8,128)S(1)}, u32[]{:S(2)}, u32[]{:S(2)}) %collective-permute-start.5) | collective-permute-done | bytes 737312 | tf_op jit(solution)/shard_map/ppermute | solution.py:19
  120.6 0.1 slice_add_fusion.1
  120.8 0.1 fusion.38
  120.8 1.1 broadcast_divide_fusion
  (46 shorter events, 0.2 us)
Async XLA Ops:
  0.0 14.3 %copy-start = (bf16[1280,1280]{1,0:T(8,128)(2,1)S(1)}, bf16[1280,1280]{1,0:T(8,128)(2,1)}, u32[]{:S(2)}) copy-start(bf16[1280,1280]{1,0:T(8,128)(2,1)} %param.34) | copy-start | bytes 9830404
  1.0 14.4 %collective-permute-start = (bf16[4,24,24]{1,2,0:T(8,128)(2,1)S(1)}, bf16[4,24,24]{1,2,0:T(8,128)(2,1)S(1)}, u32[]{:S(2)}, u32[]{:S(2)}) collective-permute-start(bf16[4,24,24]{1,2,0:T(8,128)(2,1)S(1)} %copy.36), channel_id=1, source_target_pairs={{0,254},{2,0},{4,2},{6,4},{8,6},{10,8},{12,10},{14,12},{16,14},{18... | collective-permute-start | bytes 13832 | tf_op jit(solution)/shard_map/ppermute | solution.py:19
  4.3 11.1 %collective-permute-start.1 = (bf16[4,8,24]{1,2,0:T(8,128)(2,1)S(1)}, bf16[4,8,24]{1,2,0:T(8,128)(2,1)S(1)}, u32[]{:S(2)}, u32[]{:S(2)}) collective-permute-start(bf16[4,8,24]{1,2,0:T(8,128)(2,1)S(1)} %bitcast.39), channel_id=1, source_target_pairs={{0,252},{2,254},{4,0},{6,2},{8,4},{10,6},{12,8},{14,10},{16,12},{1... | collective-permute-start | bytes 4616 | tf_op jit(solution)/shard_map/ppermute | solution.py:19
  12.1 2.8 %copy-start.4 = (f32[1280]{0:T(1024)S(1)}, f32[1280]{0:T(1024)}, u32[]{:S(2)}) copy-start(f32[1280]{0:T(1024)} %param.35) | copy-start | bytes 15364
  12.1 2.9 %copy-start.2 = (bf16[1280,320]{0,1:T(8,128)(2,1)S(1)}, bf16[1280,320]{0,1:T(8,128)(2,1)}, u32[]{:S(2)}) copy-start(bf16[1280,320]{0,1:T(8,128)(2,1)} %param.36) | copy-start | bytes 2457604
  14.3 4.0 %copy-start.9 = (s32[2]{0:T(128)S(1)}, s32[2]{0:T(128)}, u32[]{:S(2)}) copy-start(s32[2]{0:T(128)} %param.24) | copy-start | bytes 28
  14.4 8.4 %copy-start.8 = (f32[320]{0:T(512)S(1)}, f32[320]{0:T(512)}, u32[]{:S(2)}) copy-start(f32[320]{0:T(512)} %param.37) | copy-start | bytes 3844
  14.4 8.9 %copy-start.3 = (pred[8,5]{0,1:T(8,128)(4,1)S(1)}, pred[8,5]{0,1:T(8,128)(4,1)}, u32[]{:S(2)}) copy-start(pred[8,5]{0,1:T(8,128)(4,1)} %constant.110) | copy-start | bytes 124
  14.4 8.9 %copy-start.14 = (bf16[3,3,4,320]{3,2,1,0:T(4,128)(2,1)S(1)}, bf16[3,3,4,320]{3,2,1,0:T(4,128)(2,1)}, u32[]{:S(2)}) copy-start(bf16[3,3,4,320]{3,2,1,0:T(4,128)(2,1)} %param.26) | copy-start | bytes 69124
  14.4 8.9 %copy-start.15 = (f32[320]{0:T(512)S(1)}, f32[320]{0:T(512)}, u32[]{:S(2)}) copy-start(f32[320]{0:T(512)} %param.27) | copy-start | bytes 3844
  15.5 7.3 %collective-permute-start.2 = (bf16[4,56,24]{1,2,0:T(8,128)(2,1)S(1)}, bf16[4,56,24]{1,2,0:T(8,128)(2,1)S(1)}, u32[]{:S(2)}, u32[]{:S(2)}) collective-permute-start(bf16[4,56,24]{1,2,0:T(8,128)(2,1)S(1)} %pad_maximum_fusion), channel_id=1, source_target_pairs={{0,1},{1,0},{2,3},{3,2},{4,5},{5,4},{6,7},{7,6},{8,9},{9,8},{10,11... | collective-permute-start | bytes 32264 | tf_op jit(solution)/shard_map/ppermute | solution.py:19
  23.3 4.6 %copy-start.6 = (f32[320]{0:T(512)S(1)}, f32[320]{0:T(512)}, u32[]{:S(2)}) copy-start(f32[320]{0:T(512)} %param.29) | copy-start | bytes 3844
  23.3 4.6 %copy-start.7 = (f32[320]{0:T(512)S(1)}, f32[320]{0:T(512)}, u32[]{:S(2)}) copy-start(f32[320]{0:T(512)} %param.28) | copy-start | bytes 3844
  25.5 4.7 %copy-start.5 = (f32[320]{0:T(512)S(1)}, f32[320]{0:T(512)}, u32[]{:S(2)}) copy-start(f32[320]{0:T(512)} %param.31) | copy-start | bytes 3844
  28.0 2.2 %copy-start.12 = (bf16[3,3,320,320]{3,2,1,0:T(8,128)(2,1)S(1)}, bf16[3,3,320,320]{3,2,1,0:T(8,128)(2,1)}, u32[]{:S(2)}) copy-start(bf16[3,3,320,320]{3,2,1,0:T(8,128)(2,1)} %param.30) | copy-start | bytes 5529604
  35.7 2.9 %copy-start.10 = (f32[320]{0:T(512)S(1)}, f32[320]{0:T(512)}, u32[]{:S(2)}) copy-start(f32[320]{0:T(512)} %param.39) | copy-start | bytes 3844
  35.7 2.9 %copy-start.11 = (f32[320]{0:T(512)S(1)}, f32[320]{0:T(512)}, u32[]{:S(2)}) copy-start(f32[320]{0:T(512)} %param.38) | copy-start | bytes 3844
  38.1 3.1 %copy-start.16 = (f32[320]{0:T(512)S(1)}, f32[320]{0:T(512)}, u32[]{:S(2)}) copy-start(f32[320]{0:T(512)} %param.41) | copy-start | bytes 3844
  38.6 2.6 %copy-start.1 = (bf16[32,8,5,320]{3,1,2,0:T(8,128)(2,1)S(1)}, bf16[32,8,5,320]{3,1,2,0:T(8,128)(2,1)}, u32[]{:S(2)}) copy-start(bf16[32,8,5,320]{3,1,2,0:T(8,128)(2,1)} %get-tuple-element.36) | copy-start | bytes 2457604
  38.6 2.6 %copy-start.13 = (bf16[3,3,320,320]{3,2,1,0:T(8,128)(2,1)S(1)}, bf16[3,3,320,320]{3,2,1,0:T(8,128)(2,1)}, u32[]{:S(2)}) copy-start(bf16[3,3,320,320]{3,2,1,0:T(8,128)(2,1)} %param.40) | copy-start | bytes 5529604
  61.3 27.4 %collective-permute-start.3 = (f32[24,56,320]{2,1,0:T(8,128)S(1)}, f32[24,56,320]{2,1,0:T(8,128)S(1)}, u32[]{:S(2)}, u32[]{:S(2)}) collective-permute-start(f32[24,56,320]{2,1,0:T(8,128)S(1)} %slice.106), channel_id=1, source_target_pairs={{0,2},{2,4},{4,6},{6,8},{8,10},{10,12},{12,14},{14,16},{16,18},{18... | collective-permute-start | bytes 5160968 | tf_op jit(solution)/shard_map/ppermute | solution.py:19
  63.6 34.7 %collective-permute-start.4 = (bf16[8,56,320]{2,1,0:T(8,128)(2,1)S(1)}, bf16[8,56,320]{2,1,0:T(8,128)(2,1)S(1)}, u32[]{:S(2)}, u32[]{:S(2)}) collective-permute-start(bf16[8,56,320]{2,1,0:T(8,128)(2,1)S(1)} %slice.124), channel_id=1, source_target_pairs={{0,4},{2,6},{4,8},{6,10},{8,12},{10,14},{12,16},{14,18},{16,20},{1... | collective-permute-start | bytes 860168 | tf_op jit(solution)/shard_map/ppermute | solution.py:19
  98.5 22.2 %collective-permute-start.5 = (f32[24,24,320]{2,1,0:T(8,128)S(1)}, f32[24,24,320]{2,1,0:T(8,128)S(1)}, u32[]{:S(2)}, u32[]{:S(2)}) collective-permute-start(f32[24,24,320]{2,1,0:T(8,128)S(1)} %slice.110), channel_id=1, source_target_pairs={{0,1},{1,0},{2,3},{3,2},{4,5},{5,4},{6,7},{7,6},{8,9},{9,8},{10,11... | collective-permute-start | bytes 2211848 | tf_op jit(solution)/shard_map/ppermute | solution.py:19
where the time goes:
time: 122 us
  waiting for transfers between devices  53 us (43%)
  local copies, waits for them, and re-layouts  19.9 us (16%)
  starting transfers between devices  15.1 us (12%)
  matrix products  14.6 us (12%)
  other arithmetic  14.4 us (12%)
  between operations  4.94 us (4%)
    ppermute x6, waiting for transfers between devices, from_behind(): return lax.ppermute(value, axis, pairs)  53 us
    ppermute x6, starting transfers between devices, from_behind(): return lax.ppermute(value, axis, pairs)  15.1 us
    conv_general_dilated x3, matrix products, convolve(): lax.conv_general_dilated(image, kernel, (1, 1), 'SAME', dimension_numbers...  12.2 us
    dynamic_update_slice x1, local copies, waits for them, and re-layouts, on_device(): lax.dynamic_update_slice(jnp.zeros((side, side, C), jnp.float32), window_...  8.79 us
    reduce_sum x4, other arithmetic, group_norm(): var = jnp.mean((grouped - mean) ** 2, axis=(1, 2, 4), keepdims=True)  3.87 us
    convert_element_type x1, other arithmetic, on_device(): jax.nn.silu(group_norm(inner, norm_two_gain, norm_two_shift))  2.52 us
    broadcast_in_dim x1, local copies, waits for them, and re-layouts, on_device(): jnp.zeros((side, side, C), jnp.float32)  2.47 us
  transfers between devices with their start and end apart: 6, of which 3 were waited for; matrix products, arithmetic and copies ran while one was open for 7% of the time, Pallas kernels for 0%

commit v1 on v0

v1 whole, which is shorter than its diff:
```python
import functools
import math

import jax
import jax.numpy as jnp
from jax import lax
from jax.experimental import pallas as pl
from jax.experimental.pallas import tpu as pltpu
from jax.sharding import PartitionSpec as P

C = 320
TEMB = 1280
LATC = 4
GROUPS = 32
STRIDE = 24
WIN = 32
HALF = C // 2
SIZE = C // GROUPS
MAIN = 256
REST = C - MAIN
DEPTH = 3 * C
CHUNKS = 4
ROWS = WIN // CHUNKS
PIX = ROWS * WIN
EPS = 1e-05
MESH = pl.DeviceIdType.MESH
F32 = jnp.float32
BF16 = jnp.bfloat16

PLANS = {
    "low": dict(lead=0, prev=0, next=16, first=(2, 3), then=(0, 1), front=8, back=8),
    "mid": dict(lead=1, prev=16, next=0, first=(0, 1), then=(2, 3), front=8, back=8),
    "high": dict(lead=1, prev=8, next=8, first=(0, 3), then=(1, 2), front=8, back=8),
    "any": dict(lead=1, prev=24, next=8, first=(0, 1, 2, 3), then=(), front=24, back=24),
}


def silu(value):
    half = 0.5 * value
    return half * jnp.tanh(half) + half


def iota(shape, dim):
    return lax.broadcasted_iota(jnp.int32, shape, dim)


def split3(value):
    top = value.astype(BF16).astype(F32)
    left = value - top
    mid = left.astype(BF16).astype(F32)
    return jnp.concatenate([top, mid, left - mid, jnp.zeros_like(value)], axis=0).astype(BF16)


def group_sum(value, groups):
    parts = jnp.dot(split3(value), groups, preferred_element_type=F32)
    return parts[0:8] + parts[8:16] + parts[16:24]


def body(
    plan,
    row_axis,
    offsets_ref,
    timestep_ref,
    latent_ref,
    conv_in_ref,
    vec_hbm,
    tvec_hbm,
    conv_one_hbm,
    conv_two_hbm,
    time_one_hbm,
    time_two_hbm,
    time_proj_hbm,
    out_ref,
    ext,
    vec,
    tvec,
    time_one,
    time_two,
    time_proj,
    w_one,
    w_two,
    tail_one,
    tail_two,
    w_in,
    onehot,
    edge,
    cover,
    groups,
    shift_vec,
    lat,
    start,
    act,
    inner,
    band,
    means,
    spreads,
    norm_one,
    norm_two,
    send_prev,
    send_next,
    from_prev,
    from_next,
    vec_sems,
    time_sems,
    w_sems,
    lat_send,
    lat_recv,
    out_send,
    out_recv,
):
    lead, n_prev, n_next, front = plan["lead"], plan["prev"], plan["next"], plan["front"]
    row, col = lax.axis_index("rows"), lax.axis_index("cols")
    after, before = lax.rem(row + 1, row_axis), lax.rem(row + row_axis - 1, row_axis)
    other = 1 - col
    row_off = offsets_ref[0]
    col_off = offsets_ref[1]

    barrier = pltpu.get_barrier_semaphore()
    friends = [(before, col), (before, other), (row, other), (after, col), (after, other)]
    for friend in friends:
        pl.semaphore_signal(barrier, inc=1, device_id=friend, device_id_type=MESH)

    small = [
        pltpu.make_async_copy(vec_hbm, vec, vec_sems.at[0]),
        pltpu.make_async_copy(tvec_hbm, tvec, vec_sems.at[1]),
        pltpu.make_async_copy(time_one_hbm, time_one, time_sems.at[0]),
        pltpu.make_async_copy(time_two_hbm, time_two, time_sems.at[1]),
        pltpu.make_async_copy(time_proj_hbm, time_proj, time_sems.at[2]),
    ]
    for copy in small:
        copy.start()

    def weight_copies(source, target, slot):
        copies = []
        for dy in range(3):
            for dx in range(3):
                copies.append(
                    pltpu.make_async_copy(
                        source.at[dy, dx, pl.ds(0, MAIN)],
                        target.at[dy, pl.ds(dx * MAIN, MAIN)],
                        w_sems.at[slot, dy * 6 + dx * 2],
                    )
                )
                copies.append(
                    pltpu.make_async_copy(
                        source.at[dy, dx, pl.ds(MAIN, REST)],
                        target.at[dy, pl.ds(3 * MAIN + dx * REST, REST)],
                        w_sems.at[slot, dy * 6 + dx * 2 + 1],
                    )
                )
        return copies

    copies_one = weight_copies(conv_one_hbm, w_one, 0)
    copies_two = weight_copies(conv_two_hbm, w_two, 1)

    own_at = 24 * lead
    blank = jnp.zeros((STRIDE, 8), F32)
    pieces = []
    for channel in range(LATC):
        pieces += [latent_ref[channel].astype(F32), blank]
    ext[0, own_at : own_at + STRIDE, :] = jnp.concatenate(pieces, axis=1)

    pl.semaphore_wait(barrier, len(friends))

    own = ext.at[0, pl.ds(own_at, STRIDE)]
    heads = 8 if lead else 16
    head = ext.at[0, pl.ds(own_at, heads)]
    moves = [
        (own, ext.at[1, pl.ds(own_at, STRIDE)], (row, other)),
        (head, ext.at[0, pl.ds(own_at + STRIDE, heads)], (before, col)),
        (head, ext.at[1, pl.ds(own_at + STRIDE, heads)], (before, other)),
    ]
    if lead:
        moves += [
            (own, ext.at[0, pl.ds(0, STRIDE)], (after, col)),
            (own, ext.at[1, pl.ds(0, STRIDE)], (after, other)),
        ]
    lat_copies = []
    for place, (source, target, device) in enumerate(moves):
        copy = pltpu.make_async_remote_copy(
            src_ref=source,
            dst_ref=target,
            send_sem=lat_send.at[place],
            recv_sem=lat_recv.at[place],
            device_id=device,
            device_id_type=MESH,
        )
        copy.start()
        lat_copies.append(copy)
    for copy in copies_one:
        copy.start()
    for copy in copies_two:
        copy.start()

    tap = iota((MAIN, 128), 1)
    from_lane = iota((MAIN, 128), 0)
    same = ((from_lane & 127) >> 5) == (tap & 3)
    pick = jnp.where(same & (tap < 9 * LATC), 1.0, 0.0).astype(BF16)
    first_g, second_g = iota((C, C), 0), iota((C, C), 1)
    low_g = second_g - lax.rem(second_g, SIZE)
    groups[...] = jnp.where((first_g >= low_g) & (first_g < low_g + SIZE), 1.0, 0.0).astype(BF16)
    w_in[...] = jnp.zeros_like(w_in)
    w_in[0 : 9 * LATC, :] = jnp.concatenate(
        [conv_in_ref[dy, dx].astype(F32) for dy in range(3) for dx in range(3)], axis=0
    ).astype(BF16)

    slot = iota((WIN, C), 0)
    slot_wide = iota((WIN, MAIN), 0)
    lane_wide = iota((WIN, MAIN), 1)
    lane_col = lane_wide & 31
    lane_at = jnp.where(lane_col < STRIDE, (lane_wide >> 7) * STRIDE + lane_col, -100)
    for window in range(2):
        begin = col_off - 24 * window
        place = (slot_wide - begin) & 31
        column = begin + place
        column = jnp.where(column < 0, column + 48, column)
        column = jnp.where(column >= 48, column - 48, column)
        onehot[window] = jnp.where(lane_at == column, 1.0, 0.0)
        place = (slot - begin) & 31
        edge[window, 0] = jnp.where(place > 0, 1.0, 0.0)
        edge[window, 1] = jnp.where(place < WIN - 1, 1.0, 0.0)
    cover[0] = jnp.where((slot >= col_off) & (slot < STRIDE), 1.0, 0.0)
    cover[1] = jnp.where((slot <= col_off + 7) & (slot < STRIDE), 1.0, 0.0)
    cover[2] = jnp.where((slot <= col_off - 17) & (slot < 8), 1.0, 0.0)
    for window in range(2):
        lat[window, 0] = jnp.zeros((WIN, 128), F32)
        lat[window, WIN + 1] = jnp.zeros((WIN, 128), F32)
        act[window, 0] = jnp.zeros((WIN, 4 * MAIN), BF16)
        act[window, WIN + 1] = jnp.zeros((WIN, 4 * MAIN), BF16)
    band[0:front] = jnp.zeros((front, STRIDE, C), F32)
    band[front + WIN :] = jnp.zeros((plan["back"], STRIDE, C), F32)

    for copy in small:
        copy.wait()
    freq = jnp.exp(-math.log(10000.0) * iota((8, HALF), 1).astype(F32) / HALF)
    angle = timestep_ref[0].astype(F32) * freq
    cosine = jnp.concatenate([jnp.cos(angle)] * 2, axis=0).astype(BF16)
    sine = jnp.concatenate([jnp.sin(angle)] * 2, axis=0).astype(BF16)
    hidden = jnp.dot(cosine, time_one[0:HALF, :], preferred_element_type=F32)
    hidden += jnp.dot(sine, time_one[HALF:C, :], preferred_element_type=F32)
    hidden = silu(hidden + tvec[0:1, :]).astype(BF16)
    hidden = jnp.dot(hidden, time_two[...], preferred_element_type=F32)
    hidden = silu(hidden + tvec[1:2, :]).astype(BF16)
    shift = lax.dot_general(
        hidden, time_proj[...], (((1,), (1,)), ((), ())), preferred_element_type=F32
    )
    shift_vec[...] = shift[0:8] + vec[4:5, :] + vec[3:4, :]

    for copy in lat_copies:
        copy.wait()

    def place_latent(step, _):
        window, chunk = step // CHUNKS, lax.rem(step, CHUNKS)
        chosen = onehot[window]
        lines = []
        for line in range(ROWS):
            at = row_off + chunk * ROWS + line
            left = ext[0, pl.ds(at, 1), :]
            right = ext[1, pl.ds(at, 1), :]
            lines.append((jnp.concatenate([left, right], axis=1) * chosen).astype(BF16))
        spread = jnp.concatenate(lines, axis=0)
        got = jnp.dot(spread, pick, preferred_element_type=F32)
        lat[window, pl.ds(1 + chunk * ROWS, ROWS)] = got.reshape(ROWS, WIN, 128)
        return 0

    lax.fori_loop(0, 2 * CHUNKS, place_latent, 0)

    lane = iota((1, WIN, 128), 2) >> 2
    lane_row = lane // 3
    lane_col = lane - 3 * lane_row

    def keep_moments(step, value):
        mean = jnp.sum(value, axis=0, keepdims=True) * (1.0 / PIX)
        diff = value - mean
        means[step] = jnp.broadcast_to(mean, (8, C))
        spreads[step] = jnp.broadcast_to(jnp.sum(diff * diff, axis=0, keepdims=True), (8, C))

    def norm_lines(target, gain, offset):
        mean = []
        for window in range(2):
            total = means[window * CHUNKS, 0:1]
            for chunk in range(1, CHUNKS):
                total = total + means[window * CHUNKS + chunk, 0:1]
            mean.append(total * (1.0 / CHUNKS))
        spare = jnp.zeros((6, C), F32)
        centre = group_sum(jnp.concatenate(mean + [spare], axis=0), groups[...]) * (1.0 / SIZE)
        variance = []
        for window in range(2):
            total = jnp.zeros((1, C), F32)
            for chunk in range(CHUNKS):
                step = window * CHUNKS + chunk
                diff = means[step, 0:1] - centre[window : window + 1]
                total = total + spreads[step, 0:1] * (1.0 / PIX) + diff * diff
            variance.append(total * (1.0 / CHUNKS))
        var = group_sum(jnp.concatenate(variance + [spare], axis=0), groups[...]) * (1.0 / SIZE)
        scale = 0.5 * gain / jnp.sqrt(var + EPS)
        move = 0.5 * offset - centre * scale
        for window in range(2):
            target[window, 0] = jnp.broadcast_to(scale[window : window + 1], (8, C))
            target[window, 1] = jnp.broadcast_to(move[window : window + 1], (8, C))

    def run_in(step, _):
        window, chunk = step // CHUNKS, lax.rem(step, CHUNKS)
        full = lat[window, pl.ds(chunk * ROWS, ROWS + 2)]
        less = pltpu.roll(full, 1, 1) * edge[window, 0, :, 0:128]
        more = pltpu.roll(full, WIN - 1, 1) * edge[window, 1, :, 0:128]
        wide = jnp.where(lane_col == 0, less, jnp.where(lane_col == 1, full, more))
        patch = jnp.where(
            lane_row == 0,
            wide[0:ROWS],
            jnp.where(lane_row == 1, wide[1 : ROWS + 1], wide[2 : ROWS + 2]),
        )
        patch = patch.reshape(PIX, 128).astype(BF16)
        value = jnp.dot(patch, w_in[...], preferred_element_type=F32) + vec[0:1, :]
        value = value.astype(BF16)
        start[window, pl.ds(chunk * ROWS, ROWS)] = value.reshape(ROWS, WIN, C)
        keep_moments(step, value.astype(F32))
        return 0

    lax.fori_loop(0, 2 * CHUNKS, run_in, 0)
    norm_lines(norm_one, vec[1:2, :], vec[2:3, :])

    def three_columns(value, window):
        less = pltpu.roll(value, 1, 1) * edge[window, 0]
        more = pltpu.roll(value, WIN - 1, 1) * edge[window, 1]
        return less, value, more

    def store_act(window, chunk, parts):
        at = pl.ds(1 + chunk * ROWS, ROWS)
        for place, part in enumerate(parts):
            act[window, at, :, place * MAIN : (place + 1) * MAIN] = part[:, :, 0:MAIN].astype(BF16)
        rest = jnp.concatenate([part[:, :, MAIN:C] for part in parts], axis=2)
        act[window, at, :, 3 * MAIN : DEPTH] = rest.astype(BF16)

    def activate(value, lines, window):
        half = value * lines[window, 0, 0:1] + lines[window, 1, 0:1]
        return half * jnp.tanh(half) + half

    def run_act(step, _):
        window, chunk = step // CHUNKS, lax.rem(step, CHUNKS)
        value = start[window, pl.ds(chunk * ROWS, ROWS)].astype(F32)
        value = activate(value, norm_one, window)
        store_act(window, chunk, three_columns(value, window))
        return 0

    lax.fori_loop(0, 2 * CHUNKS, run_act, 0)

    def tails(weights, target):
        blocks = [weights[dy, :, MAIN:C] for dy in range(3)]
        target[...] = jnp.concatenate(blocks, axis=1)

    def convolve(window, chunk, weights, tail):
        wide = act[window, pl.ds(chunk * ROWS, ROWS + 2), :, 0:DEPTH]
        wide = wide.reshape((ROWS + 2) * WIN, DEPTH)
        total = jnp.dot(wide[0:PIX], weights[0, :, 0:MAIN], preferred_element_type=F32)
        total += jnp.dot(wide[WIN : WIN + PIX], weights[1, :, 0:MAIN], preferred_element_type=F32)
        total += jnp.dot(wide[2 * WIN :], weights[2, :, 0:MAIN], preferred_element_type=F32)
        rest = jnp.dot(wide, tail[...], preferred_element_type=F32)
        left = (
            rest[0:PIX, 0:REST]
            + rest[WIN : WIN + PIX, REST : 2 * REST]
            + rest[2 * WIN :, 2 * REST : 3 * REST]
        )
        return jnp.concatenate([total, left], axis=1)

    for copy in copies_one:
        copy.wait()
    tails(w_one, tail_one)

    def run_one(step, _):
        window, chunk = step // CHUNKS, lax.rem(step, CHUNKS)
        value = convolve(window, chunk, w_one, tail_one) + shift_vec[0:1, :]
        inner[window, pl.ds(chunk * ROWS, ROWS)] = value.reshape(ROWS, WIN, C)
        keep_moments(step, value)
        return 0

    lax.fori_loop(0, 2 * CHUNKS, run_one, 0)
    norm_lines(norm_two, vec[5:6, :], vec[6:7, :])

    def merge(first, second):
        main = first * cover[0] + second * cover[1]
        wrap = first[:, 16:24] * cover[2, 0:8]
        return jnp.concatenate([main[:, 0:8] + wrap, main[:, 8:WIN]], axis=1)

    def run_merge(chunk, _):
        lines = []
        for window in range(2):
            value = inner[window, pl.ds(chunk * ROWS, ROWS)]
            value = activate(value, norm_two, window).astype(BF16).astype(F32)
            lines.append(three_columns(value, window))
        store_act(0, chunk, [merge(lines[0][place], lines[1][place]) for place in range(3)])
        return 0

    lax.fori_loop(0, CHUNKS, run_merge, 0)

    for copy in copies_two:
        copy.wait()
    tails(w_two, tail_two)
    counted = cover[0] + cover[1]
    counted = jnp.concatenate([counted[0:8] + cover[2, 0:8], counted[8:STRIDE]], axis=0)

    def run_two(chunk):
        value = convolve(0, chunk, w_two, tail_two).reshape(ROWS, WIN, C)
        at = pl.ds(chunk * ROWS, ROWS)
        first, second = start[0, at].astype(F32), start[1, at].astype(F32)
        value = (value + merge(first, second))[:, 0:STRIDE] + counted * vec[7:8, :]
        band[pl.ds(front + chunk * ROWS, ROWS)] = value

    def run_chunks(chunks):
        if len(chunks) == 0:
            return
        step = chunks[1] - chunks[0]

        def one(index, _):
            run_two(chunks[0] + index * step)
            return 0

        lax.fori_loop(0, len(chunks), one, 0)

    run_chunks(plan["first"])

    def stage(target, base, count):
        def one(pair, _):
            upper = band[base + 2 * pair]
            lower = band[base + 2 * pair + 1]
            target[pair] = jnp.concatenate([upper, lower], axis=0).astype(BF16)
            return 0

        lax.fori_loop(0, count // 2, one, 0)

    out_copies = []
    if n_prev:
        stage(send_prev, front + 24 * lead - row_off - n_prev, n_prev)
        out_copies.append((send_prev, from_next, (before, col), 0))
    if n_next:
        stage(send_next, front + 24 + 24 * lead - row_off, n_next)
        out_copies.append((send_next, from_prev, (after, col), 1))
    started = []
    for source, target, device, place in out_copies:
        copy = pltpu.make_async_remote_copy(
            src_ref=source,
            dst_ref=target,
            send_sem=out_send.at[place],
            recv_sem=out_recv.at[place],
            device_id=device,
            device_id_type=MESH,
        )
        copy.start()
        started.append(copy)

    run_chunks(plan["then"])
    for copy in started:
        copy.wait()

    scale_cols = 1.0 / counted

    def finish(pair, has_prev, has_next):
        pieces = []
        for line in range(2):
            at = 2 * pair + line
            pieces.append(band[front + 24 * lead - row_off + at])
        value = jnp.concatenate(pieces, axis=0)
        if has_prev:
            value = value + from_prev[pair].astype(F32)
        if has_next:
            value = value + from_next[pair - (STRIDE - n_prev) // 2].astype(F32)
        for line in range(2):
            at = 2 * pair + line
            twice = lax.rem(at - row_off + 24, 24) < 8
            scale = jnp.where(twice, 0.5, 1.0)
            out_ref[at] = value[line * STRIDE : (line + 1) * STRIDE] * (scale_cols * scale)

    marks = sorted({0, n_next // 2, (STRIDE - n_prev) // 2, STRIDE // 2})
    for low, high in zip(marks[:-1], marks[1:]):
        has_prev = low < n_next // 2
        has_next = low >= (STRIDE - n_prev) // 2

        def one(pair, _, has_prev=has_prev, has_next=has_next):
            finish(pair, has_prev, has_next)
            return 0

        lax.fori_loop(low, high, one, 0)


def block_kernel(name, row_axis, ident, operands):
    plan = PLANS[name]
    hbm = pl.BlockSpec(memory_space=pl.ANY)
    smem = pl.BlockSpec(memory_space=pltpu.SMEM)
    vmem = pl.BlockSpec(memory_space=pltpu.VMEM)
    n_prev, n_next = max(plan["prev"], 2), max(plan["next"], 2)
    ext_rows = 56 if plan["lead"] else 40
    band_rows = plan["front"] + WIN + plan["back"]
    scratch = [
        pltpu.VMEM((2, ext_rows, 128), F32),
        pltpu.VMEM((8, C), F32),
        pltpu.VMEM((2, TEMB), F32),
        pltpu.VMEM((C, TEMB), BF16),
        pltpu.VMEM((TEMB, TEMB), BF16),
        pltpu.VMEM((C, TEMB), BF16),
        pltpu.VMEM((3, DEPTH, C), BF16),
        pltpu.VMEM((3, DEPTH, C), BF16),
        pltpu.VMEM((DEPTH, 3 * REST), BF16),
        pltpu.VMEM((DEPTH, 3 * REST), BF16),
        pltpu.VMEM((128, C), BF16),
        pltpu.VMEM((2, WIN, MAIN), F32),
        pltpu.VMEM((2, 2, WIN, C), F32),
        pltpu.VMEM((3, WIN, C), F32),
        pltpu.VMEM((C, C), BF16),
        pltpu.VMEM((8, C), F32),
        pltpu.VMEM((2, WIN + 2, WIN, 128), F32),
        pltpu.VMEM((2, WIN, WIN, C), BF16),
        pltpu.VMEM((2, WIN + 2, WIN, 4 * MAIN), BF16),
        pltpu.VMEM((2, WIN, WIN, C), F32),
        pltpu.VMEM((band_rows, STRIDE, C), F32),
        pltpu.VMEM((2 * CHUNKS, 8, C), F32),
        pltpu.VMEM((2 * CHUNKS, 8, C), F32),
        pltpu.VMEM((2, 2, 8, C), F32),
        pltpu.VMEM((2, 2, 8, C), F32),
        pltpu.VMEM((n_prev // 2, 2 * STRIDE, C), BF16),
        pltpu.VMEM((n_next // 2, 2 * STRIDE, C), BF16),
        pltpu.VMEM((n_next // 2, 2 * STRIDE, C), BF16),
        pltpu.VMEM((n_prev // 2, 2 * STRIDE, C), BF16),
        pltpu.SemaphoreType.DMA((2,)),
        pltpu.SemaphoreType.DMA((3,)),
        pltpu.SemaphoreType.DMA((2, 18)),
        pltpu.SemaphoreType.DMA((5,)),
        pltpu.SemaphoreType.DMA((5,)),
        pltpu.SemaphoreType.DMA((2,)),
        pltpu.SemaphoreType.DMA((2,)),
    ]
    return pl.pallas_call(
        functools.partial(body, plan, row_axis),
        out_shape=jax.ShapeDtypeStruct((STRIDE, STRIDE, C), F32),
        in_specs=[smem, smem, vmem, vmem] + [hbm] * 7,
        out_specs=vmem,
        scratch_shapes=scratch,
        compiler_params=pltpu.CompilerParams(
            collective_id=ident, has_side_effects=True, vmem_limit_bytes=56 * 1024 * 1024
        ),
        cost_estimate=pl.CostEstimate(
            flops=3 * 2 * 1024 * 2880 * 320, bytes_accessed=10**7, transcendentals=10**6
        ),
        name="panorama_block",
    )(*operands)


def on_device(
    row_axis,
    latent,
    offsets,
    timestep,
    conv_in_weight,
    conv_in_bias,
    norm_one_gain,
    norm_one_shift,
    conv_one_weight,
    conv_one_bias,
    time_one_weight,
    time_one_bias,
    time_two_weight,
    time_two_bias,
    time_proj_weight,
    time_proj_bias,
    norm_two_gain,
    norm_two_shift,
    conv_two_weight,
    conv_two_bias,
):
    vec = jnp.stack(
        [
            conv_in_bias,
            norm_one_gain,
            norm_one_shift,
            conv_one_bias,
            time_proj_bias,
            norm_two_gain,
            norm_two_shift,
            conv_two_bias,
        ]
    )
    tvec = jnp.stack([time_one_bias, time_two_bias])
    operands = (
        offsets,
        timestep,
        latent,
        conv_in_weight,
        vec,
        tvec,
        conv_one_weight,
        conv_two_weight,
        time_one_weight,
        time_two_weight,
        time_proj_weight.T,
    )
    return block_kernel("any", row_axis, 0, operands)


def solution(mesh):
    return jax.shard_map(
        functools.partial(on_device, mesh.shape["rows"]),
        mesh=mesh,
        in_specs=(P(None, "rows", "cols"),) + (P(),) * 18,
        out_specs=P("rows", "cols", None),
        check_vma=False,
    )
```

time: 122 us -> 54.2 us (0.44)
  the two profiles are of different devices: /device:TPU:1 before, /device:TPU:16 now
where the time goes in v1:
time: 54.2 us; the launch traced here: 53.8 us
  Pallas kernels  42.9 us (79%)
  local copies, waits for them, and re-layouts  9.62 us (18%)
  between operations  0.67 us (1%)
  other arithmetic  0.6 us (1%)
    pallas_call x1, Pallas kernels, block_kernel(): pl.pallas_call(functools.partial(body, plan, row_axis), out_shape=jax.Sha...  42.9 us
    another operation x9, local copies, waits for them, and re-layouts, on_device(): jnp.stack([conv_in_bias, norm_one_gain, norm_one_shift, conv_one_bias, ti...  6.09 us
    unnamed x1, local copies, waits for them, and re-layouts  2.14 us
    another operation x2, local copies, waits for them, and re-layouts, on_device(): tvec = jnp.stack([time_one_bias, time_two_bias])  1.4 us

profile of v1, /device:TPU:16, one launch (start us, length us, event | category | flops | bytes accessed | tf_op | source)
XLA Modules:
  0.0 53.8 jit_solution(12323111518294773333)
XLA Ops:
  0.7 0.7 %stack.36 = f32[1,320]{1,0:T(1,128)S(1)} reshape(f32[320]{0:T(512)} %param.23) | data formatting | bytes 2560 | tf_op jit(solution)/shard_map/stack | solution.py:569
  1.3 0.7 %stack.37 = f32[1,320]{1,0:T(1,128)S(1)} reshape(f32[320]{0:T(512)} %param.24) | data formatting | bytes 2560 | tf_op jit(solution)/shard_map/stack | solution.py:569
  2.0 0.7 %stack.38 = f32[1,320]{1,0:T(1,128)S(1)} reshape(f32[320]{0:T(512)} %param.25) | data formatting | bytes 2560 | tf_op jit(solution)/shard_map/stack | solution.py:569
  2.7 0.7 %stack.39 = f32[1,320]{1,0:T(1,128)S(1)} reshape(f32[320]{0:T(512)} %param.27) | data formatting | bytes 2560 | tf_op jit(solution)/shard_map/stack | solution.py:569
  3.4 0.7 %stack.40 = f32[1,320]{1,0:T(1,128)S(1)} reshape(f32[320]{0:T(512)} %param.33) | data formatting | bytes 2560 | tf_op jit(solution)/shard_map/stack | solution.py:569
  4.1 0.7 %stack.41 = f32[1,320]{1,0:T(1,128)S(1)} reshape(f32[320]{0:T(512)} %param.34) | data formatting | bytes 2560 | tf_op jit(solution)/shard_map/stack | solution.py:569
  4.8 0.7 %stack.42 = f32[1,320]{1,0:T(1,128)S(1)} reshape(f32[320]{0:T(512)} %param.35) | data formatting | bytes 2560 | tf_op jit(solution)/shard_map/stack | solution.py:569
  5.4 0.7 %stack.43 = f32[1,320]{1,0:T(1,128)S(1)} reshape(f32[320]{0:T(512)} %param.37) | data formatting | bytes 2560 | tf_op jit(solution)/shard_map/stack | solution.py:569
  6.1 0.6 %stack.44.vec_hbm = f32[8,320]{1,0:T(8,128)} concatenate(f32[1,320]{1,0:T(1,128)S(1)} %stack.36, f32[1,320]{1,0:T(1,128)S(1)} %stack.37, f32[1,320]{1,0:T(1,128)S(1)} %stack.38, f32[1,320]{1,0:T(1,128)S(1)} %stack.39, f32[1,320]{1,0:T(1,128)S(1)} %stack.40, f32[1,320]{1,0:T(1,128)S(1)} %stack.41, f32[1,320]{1,0:T(1,128)S(1)} %stack.42, f32[1,320]{1,0:T(1,128)S(1)} %stack.43), dimensions={0} | concatenate | bytes 20480 | tf_op jit(solution)/shard_map/stack | solution.py:569
  6.7 0.7 %stack.45 = f32[1,1280]{1,0:T(1,128)S(1)} reshape(f32[1280]{0:T(1024)} %param.29) | data formatting | bytes 10240 | tf_op jit(solution)/shard_map/stack | solution.py:581
  7.4 0.7 %stack.46 = f32[1,1280]{1,0:T(1,128)S(1)} reshape(f32[1280]{0:T(1024)} %param.31) | data formatting | bytes 10240 | tf_op jit(solution)/shard_map/stack | solution.py:581
  8.1 0.6 %pad_maximum_fusion.tvec_hbm = f32[2,1280]{1,0:T(2,128)} fusion(f32[1,1280]{1,0:T(1,128)S(1)} %stack.46, f32[1,1280]{1,0:T(1,128)S(1)} %stack.45), kind=kLoop, calls=%fused_computation | loop fusion | flops 2560 | bytes 20480 | tf_op jit(solution)/shard_map/stack | solution.py:581
  8.7 42.9 %panorama_block.1 = f32[24,24,320]{2,1,0:T(8,128)} custom-call(s32[2]{0:T(128)} %offsets_ref.1, s32[1]{0:T(128)S(6)} %copy.21.timestep_ref, bf16[4,24,24]{2,1,0:T(8,128)(2,1)} %latent_ref.1, bf16[3,3,4,320]{3,2,1,0:T(4,128)(2,1)} %conv_in_ref.1, f32[8,320]{1,0:T(8,128)} %stack.44.vec_hbm, f32[2,1280]{1,0:T(2,128)} %pad_maximum_fusion.tvec_hbm, ...), custom_call_target="tpu_custom_call" | custom-call | flops 5662310400 | bytes 10000000 | tf_op jit(solution)/shard_map/panorama_block/pallas_call | solution.py:531
  51.6 2.1 %copy.22 = f32[24,24,320]{2,1,0:T(8,128)} copy(f32[24,24,320]{2,1,0:T(8,128)} %panorama_block.1) | data formatting | bytes 1474560

commit v2 on v1

--- a/solution.py
+++ b/solution.py
@@ -21,17 +21,18 @@
 DEPTH = 3 * C
 CHUNKS = 4
 ROWS = WIN // CHUNKS
-PIX = ROWS * WIN
 EPS = 1e-05
+AREA = WIN * WIN
 MESH = pl.DeviceIdType.MESH
 F32 = jnp.float32
 BF16 = jnp.bfloat16
 
 PLANS = {
-    "low": dict(lead=0, prev=0, next=16, first=(2, 3), then=(0, 1), front=8, back=8),
-    "mid": dict(lead=1, prev=16, next=0, first=(0, 1), then=(2, 3), front=8, back=8),
-    "high": dict(lead=1, prev=8, next=8, first=(0, 3), then=(1, 2), front=8, back=8),
-    "any": dict(lead=1, prev=24, next=8, first=(0, 1, 2, 3), then=(), front=24, back=24),
+    "low": dict(low=0, lead=0, prev=0, next=16, first=[(8, 8)], then=[(0, 8)], front=8, back=8),
+    "mid": dict(low=8, lead=1, prev=16, next=0, first=[(0, 8)], then=[(8, 8)], front=8, back=8),
+    "high": dict(
+        low=16, lead=1, prev=8, next=8, first=[(0, 4), (12, 4)], then=[(4, 8)], front=8, back=8
+    ),
 }
 
 
@@ -59,21 +60,41 @@
 def body(
     plan,
     row_axis,
-    offsets_ref,
-    timestep_ref,
-    latent_ref,
-    conv_in_ref,
-    vec_hbm,
-    tvec_hbm,
+    offsets_hbm,
+    timestep_hbm,
+    latent_hbm,
+    conv_in_hbm,
+    conv_in_bias_hbm,
+    gain_one_hbm,
+    move_one_hbm,
+    conv_one_bias_hbm,
+    proj_bias_hbm,
+    gain_two_hbm,
+    move_two_hbm,
+    conv_two_bias_hbm,
+    time_one_bias_hbm,
+    time_two_bias_hbm,
     conv_one_hbm,
     conv_two_hbm,
     time_one_hbm,
     time_two_hbm,
     time_proj_hbm,
     out_ref,
+    offsets_ref,
+    timestep_ref,
+    latent_ref,
+    conv_in_ref,
     ext,
-    vec,
-    tvec,
+    conv_in_bias,
+    gain_one,
+    move_one,
+    conv_one_bias,
+    proj_bias,
+    gain_two,
+    move_two,
+    conv_two_bias,
+    time_one_bias,
+    time_two_bias,
     time_one,
     time_two,
     time_proj,
@@ -85,12 +106,16 @@
     onehot,
     edge,
     cover,
+    wrap,
     groups,
     shift_vec,
     lat,
     start,
     act,
     inner,
+    last,
+    even,
+    odd,
     band,
     means,
     spreads,
@@ -100,6 +125,7 @@
     send_next,
     from_prev,
     from_next,
+    in_sems,
     vec_sems,
     time_sems,
     w_sems,
@@ -112,23 +138,43 @@
     row, col = lax.axis_index("rows"), lax.axis_index("cols")
     after, before = lax.rem(row + 1, row_axis), lax.rem(row + row_axis - 1, row_axis)
     other = 1 - col
-    row_off = offsets_ref[0]
-    col_off = offsets_ref[1]
-
     barrier = pltpu.get_barrier_semaphore()
     friends = [(before, col), (before, other), (row, other), (after, col), (after, other)]
     for friend in friends:
         pl.semaphore_signal(barrier, inc=1, device_id=friend, device_id_type=MESH)
 
+    arguments = [
+        pltpu.make_async_copy(latent_hbm, latent_ref, in_sems.at[0]),
+        pltpu.make_async_copy(offsets_hbm, offsets_ref, in_sems.at[1]),
+        pltpu.make_async_copy(timestep_hbm, timestep_ref, in_sems.at[2]),
+        pltpu.make_async_copy(conv_in_hbm, conv_in_ref, in_sems.at[3]),
+    ]
+    for copy in arguments:
+        copy.start()
     small = [
-        pltpu.make_async_copy(vec_hbm, vec, vec_sems.at[0]),
-        pltpu.make_async_copy(tvec_hbm, tvec, vec_sems.at[1]),
         pltpu.make_async_copy(time_one_hbm, time_one, time_sems.at[0]),
         pltpu.make_async_copy(time_two_hbm, time_two, time_sems.at[1]),
         pltpu.make_async_copy(time_proj_hbm, time_proj, time_sems.at[2]),
     ]
+    vectors = [
+        (conv_in_bias_hbm, conv_in_bias),
+        (gain_one_hbm, gain_one),
+        (move_one_hbm, move_one),
+        (conv_one_bias_hbm, conv_one_bias),
+        (proj_bias_hbm, proj_bias),
+        (gain_two_hbm, gain_two),
+        (move_two_hbm, move_two),
+        (conv_two_bias_hbm, conv_two_bias),
+        (time_one_bias_hbm, time_one_bias),
+        (time_two_bias_hbm, time_two_bias),
+    ]
+    for place, (source, target) in enumerate(vectors):
+        small.append(pltpu.make_async_copy(source, target, vec_sems.at[place]))
     for copy in small:
         copy.start()
+
+    def line_of(ref):
+        return ref[...].reshape(1, ref.shape[0])
 
     def weight_copies(source, target, slot):
         copies = []
@@ -152,6 +198,11 @@
 
     copies_one = weight_copies(conv_one_hbm, w_one, 0)
     copies_two = weight_copies(conv_two_hbm, w_two, 1)
+
+    for copy in arguments:
+        copy.wait()
+    row_off = jnp.clip(offsets_ref[0], plan["low"], plan["low"] + 7)
+    col_off = offsets_ref[1]
 
     own_at = 24 * lead
     blank = jnp.zeros((STRIDE, 8), F32)
@@ -219,14 +270,25 @@
         place = (slot - begin) & 31
         edge[window, 0] = jnp.where(place > 0, 1.0, 0.0)
         edge[window, 1] = jnp.where(place < WIN - 1, 1.0, 0.0)
-    cover[0] = jnp.where((slot >= col_off) & (slot < STRIDE), 1.0, 0.0)
-    cover[1] = jnp.where((slot <= col_off + 7) & (slot < STRIDE), 1.0, 0.0)
-    cover[2] = jnp.where((slot <= col_off - 17) & (slot < 8), 1.0, 0.0)
+    mine = iota((STRIDE, C), 0)
+    near = iota((8, C), 0)
+    for tap in range(3):
+        for window in range(2):
+            covered = (mine >= col_off) if window == 0 else (mine <= col_off + 7)
+            mask = jnp.where(covered, 1.0, 0.0)
+            if tap != 1:
+                mask = mask * edge[window, tap // 2, 0:STRIDE]
+            cover[window, tap] = mask
+        mask = jnp.where(near <= col_off - 17, 1.0, 0.0)
+        if tap != 1:
+            mask = mask * edge[0, tap // 2, 16:24]
+        wrap[tap] = mask
     for window in range(2):
         lat[window, 0] = jnp.zeros((WIN, 128), F32)
         lat[window, WIN + 1] = jnp.zeros((WIN, 128), F32)
         act[window, 0] = jnp.zeros((WIN, 4 * MAIN), BF16)
         act[window, WIN + 1] = jnp.zeros((WIN, 4 * MAIN), BF16)
+    last[...] = jnp.zeros_like(last)
     band[0:front] = jnp.zeros((front, STRIDE, C), F32)
     band[front + WIN :] = jnp.zeros((plan["back"], STRIDE, C), F32)
 
@@ -238,99 +300,83 @@
     sine = jnp.concatenate([jnp.sin(angle)] * 2, axis=0).astype(BF16)
     hidden = jnp.dot(cosine, time_one[0:HALF, :], preferred_element_type=F32)
     hidden += jnp.dot(sine, time_one[HALF:C, :], preferred_element_type=F32)
-    hidden = silu(hidden + tvec[0:1, :]).astype(BF16)
+    hidden = silu(hidden + line_of(time_one_bias)).astype(BF16)
     hidden = jnp.dot(hidden, time_two[...], preferred_element_type=F32)
-    hidden = silu(hidden + tvec[1:2, :]).astype(BF16)
+    hidden = silu(hidden + line_of(time_two_bias)).astype(BF16)
     shift = lax.dot_general(
         hidden, time_proj[...], (((1,), (1,)), ((), ())), preferred_element_type=F32
     )
-    shift_vec[...] = shift[0:8] + vec[4:5, :] + vec[3:4, :]
+    shift_vec[...] = shift[0:8] + line_of(proj_bias) + line_of(conv_one_bias)
 
     for copy in lat_copies:
-        copy.wait()
-
-    def place_latent(step, _):
-        window, chunk = step // CHUNKS, lax.rem(step, CHUNKS)
-        chosen = onehot[window]
-        lines = []
-        for line in range(ROWS):
-            at = row_off + chunk * ROWS + line
-            left = ext[0, pl.ds(at, 1), :]
-            right = ext[1, pl.ds(at, 1), :]
-            lines.append((jnp.concatenate([left, right], axis=1) * chosen).astype(BF16))
-        spread = jnp.concatenate(lines, axis=0)
-        got = jnp.dot(spread, pick, preferred_element_type=F32)
-        lat[window, pl.ds(1 + chunk * ROWS, ROWS)] = got.reshape(ROWS, WIN, 128)
-        return 0
-
-    lax.fori_loop(0, 2 * CHUNKS, place_latent, 0)
+        copy.wait_recv()
 
     lane = iota((1, WIN, 128), 2) >> 2
     lane_row = lane // 3
     lane_col = lane - 3 * lane_row
 
-    def keep_moments(step, value):
-        mean = jnp.sum(value, axis=0, keepdims=True) * (1.0 / PIX)
+    def keep_moments(window, value):
+        mean = jnp.sum(value, axis=0, keepdims=True) * (1.0 / AREA)
         diff = value - mean
-        means[step] = jnp.broadcast_to(mean, (8, C))
-        spreads[step] = jnp.broadcast_to(jnp.sum(diff * diff, axis=0, keepdims=True), (8, C))
+        means[window] = jnp.broadcast_to(mean, (8, C))
+        spread = jnp.sum(diff * diff, axis=0, keepdims=True) * (1.0 / AREA)
+        spreads[window] = jnp.broadcast_to(spread, (8, C))
 
     def norm_lines(target, gain, offset):
-        mean = []
-        for window in range(2):
-            total = means[window * CHUNKS, 0:1]
-            for chunk in range(1, CHUNKS):
-                total = total + means[window * CHUNKS + chunk, 0:1]
-            mean.append(total * (1.0 / CHUNKS))
         spare = jnp.zeros((6, C), F32)
-        centre = group_sum(jnp.concatenate(mean + [spare], axis=0), groups[...]) * (1.0 / SIZE)
-        variance = []
-        for window in range(2):
-            total = jnp.zeros((1, C), F32)
-            for chunk in range(CHUNKS):
-                step = window * CHUNKS + chunk
-                diff = means[step, 0:1] - centre[window : window + 1]
-                total = total + spreads[step, 0:1] * (1.0 / PIX) + diff * diff
-            variance.append(total * (1.0 / CHUNKS))
-        var = group_sum(jnp.concatenate(variance + [spare], axis=0), groups[...]) * (1.0 / SIZE)
+        mean = jnp.concatenate([means[0, 0:1], means[1, 0:1], spare], axis=0)
+        spread = jnp.concatenate([spreads[0, 0:1], spreads[1, 0:1], spare], axis=0)
+        centre = group_sum(mean, groups[...]) * (1.0 / SIZE)
+        diff = mean - centre
+        var = group_sum(spread + diff * diff, groups[...]) * (1.0 / SIZE)
         scale = 0.5 * gain / jnp.sqrt(var + EPS)
         move = 0.5 * offset - centre * scale
         for window in range(2):
             target[window, 0] = jnp.broadcast_to(scale[window : window + 1], (8, C))
             target[window, 1] = jnp.broadcast_to(move[window : window + 1], (8, C))
 
-    def run_in(step, _):
-        window, chunk = step // CHUNKS, lax.rem(step, CHUNKS)
-        full = lat[window, pl.ds(chunk * ROWS, ROWS + 2)]
+    def run_in(window, _):
+        chosen = onehot[window]
+        lines = []
+        for line in range(WIN):
+            at = row_off + line
+            left = ext[0, pl.ds(at, 1), :]
+            right = ext[1, pl.ds(at, 1), :]
+            lines.append((jnp.concatenate([left, right], axis=1) * chosen).astype(BF16))
+        got = jnp.dot(jnp.concatenate(lines, axis=0), pick, preferred_element_type=F32)
+        lat[window, 1 : WIN + 1] = got.reshape(WIN, WIN, 128)
+        full = lat[window]
         less = pltpu.roll(full, 1, 1) * edge[window, 0, :, 0:128]
         more = pltpu.roll(full, WIN - 1, 1) * edge[window, 1, :, 0:128]
         wide = jnp.where(lane_col == 0, less, jnp.where(lane_col == 1, full, more))
         patch = jnp.where(
             lane_row == 0,
-            wide[0:ROWS],
-            jnp.where(lane_row == 1, wide[1 : ROWS + 1], wide[2 : ROWS + 2]),
+            wide[0:WIN],
+            jnp.where(lane_row == 1, wide[1 : WIN + 1], wide[2 : WIN + 2]),
         )
-        patch = patch.reshape(PIX, 128).astype(BF16)
-        value = jnp.dot(patch, w_in[...], preferred_element_type=F32) + vec[0:1, :]
+        patch = patch.reshape(AREA, 128).astype(BF16)
+        value = jnp.dot(patch, w_in[...], preferred_element_type=F32) + line_of(conv_in_bias)
         value = value.astype(BF16)
-        start[window, pl.ds(chunk * ROWS, ROWS)] = value.reshape(ROWS, WIN, C)
-        keep_moments(step, value.astype(F32))
+        start[window] = value.reshape(WIN, WIN, C)
+        keep_moments(window, value.astype(F32))
         return 0
 
-    lax.fori_loop(0, 2 * CHUNKS, run_in, 0)
-    norm_lines(norm_one, vec[1:2, :], vec[2:3, :])
+    lax.fori_loop(0, 2, run_in, 0)
+    norm_lines(norm_one, line_of(gain_one), line_of(move_one))
 
     def three_columns(value, window):
         less = pltpu.roll(value, 1, 1) * edge[window, 0]
         more = pltpu.roll(value, WIN - 1, 1) * edge[window, 1]
         return less, value, more
 
+    def rests(parts):
+        return jnp.concatenate([part[..., MAIN:C] for part in parts], axis=-1).astype(BF16)
+
     def store_act(window, chunk, parts):
         at = pl.ds(1 + chunk * ROWS, ROWS)
         for place, part in enumerate(parts):
             act[window, at, :, place * MAIN : (place + 1) * MAIN] = part[:, :, 0:MAIN].astype(BF16)
-        rest = jnp.concatenate([part[:, :, MAIN:C] for part in parts], axis=2)
-        act[window, at, :, 3 * MAIN : DEPTH] = rest.astype(BF16)
+        act[window, at, :, 3 * MAIN : DEPTH] = rests(parts)
 
     def activate(value, lines, window):
         half = value * lines[window, 0, 0:1] + lines[window, 1, 0:1]
@@ -349,17 +395,16 @@
         blocks = [weights[dy, :, MAIN:C] for dy in range(3)]
         target[...] = jnp.concatenate(blocks, axis=1)
 
-    def convolve(window, chunk, weights, tail):
-        wide = act[window, pl.ds(chunk * ROWS, ROWS + 2), :, 0:DEPTH]
-        wide = wide.reshape((ROWS + 2) * WIN, DEPTH)
-        total = jnp.dot(wide[0:PIX], weights[0, :, 0:MAIN], preferred_element_type=F32)
-        total += jnp.dot(wide[WIN : WIN + PIX], weights[1, :, 0:MAIN], preferred_element_type=F32)
-        total += jnp.dot(wide[2 * WIN :], weights[2, :, 0:MAIN], preferred_element_type=F32)
-        rest = jnp.dot(wide, tail[...], preferred_element_type=F32)
+    def taps(sources, whole, width, weights, tail):
+        pixels = sources[0].shape[0]
+        total = jnp.dot(sources[0], weights[0, :, 0:MAIN], preferred_element_type=F32)
+        total += jnp.dot(sources[1], weights[1, :, 0:MAIN], preferred_element_type=F32)
+        total += jnp.dot(sources[2], weights[2, :, 0:MAIN], preferred_element_type=F32)
+        rest = jnp.dot(whole, tail[...], preferred_element_type=F32)
         left = (
-            rest[0:PIX, 0:REST]
-            + rest[WIN : WIN + PIX, REST : 2 * REST]
-            + rest[2 * WIN :, 2 * REST : 3 * REST]
+            rest[0:pixels, 0:REST]
+            + rest[width : width + pixels, REST : 2 * REST]
+            + rest[2 * width : 2 * width + pixels, 2 * REST : 3 * REST]
         )
         return jnp.concatenate([total, left], axis=1)
 
@@ -367,57 +412,69 @@
         copy.wait()
     tails(w_one, tail_one)
 
-    def run_one(step, _):
-        window, chunk = step // CHUNKS, lax.rem(step, CHUNKS)
-        value = convolve(window, chunk, w_one, tail_one) + shift_vec[0:1, :]
-        inner[window, pl.ds(chunk * ROWS, ROWS)] = value.reshape(ROWS, WIN, C)
-        keep_moments(step, value)
+    def run_one(window, _):
+        sources = [act[window, dy : dy + WIN, :, 0:DEPTH].reshape(AREA, DEPTH) for dy in range(3)]
+        whole = act[window, :, :, 0:DEPTH].reshape((WIN + 2) * WIN, DEPTH)
+        value = taps(sources, whole, WIN, w_one, tail_one) + shift_vec[0:1, :]
+        inner[window] = value.reshape(WIN, WIN, C)
+        keep_moments(window, value)
         return 0
 
-    lax.fori_loop(0, 2 * CHUNKS, run_one, 0)
-    norm_lines(norm_two, vec[5:6, :], vec[6:7, :])
-
-    def merge(first, second):
-        main = first * cover[0] + second * cover[1]
-        wrap = first[:, 16:24] * cover[2, 0:8]
-        return jnp.concatenate([main[:, 0:8] + wrap, main[:, 8:WIN]], axis=1)
+    lax.fori_loop(0, 2, run_one, 0)
+    norm_lines(norm_two, line_of(gain_two), line_of(move_two))
+
+    def merge(first, second, tap):
+        main = first[:, 0:STRIDE] * cover[0, tap] + second[:, 0:STRIDE] * cover[1, tap]
+        extra = first[:, 16:24] * wrap[tap]
+        return jnp.concatenate([main[:, 0:8] + extra, main[:, 8:STRIDE]], axis=1)
+
+    def store_pairs(target, at, count, parts):
+        parts = [part.reshape(count, 2 * STRIDE, C) for part in parts]
+        for place, part in enumerate(parts):
+            target[at, :, place * MAIN : (place + 1) * MAIN] = part[:, :, 0:MAIN].astype(BF16)
+        target[at, :, 3 * MAIN : DEPTH] = rests(parts)
 
     def run_merge(chunk, _):
         lines = []
         for window in range(2):
             value = inner[window, pl.ds(chunk * ROWS, ROWS)]
             value = activate(value, norm_two, window).astype(BF16).astype(F32)
-            lines.append(three_columns(value, window))
-        store_act(0, chunk, [merge(lines[0][place], lines[1][place]) for place in range(3)])
+            lines.append((pltpu.roll(value, 1, 1), value, pltpu.roll(value, WIN - 1, 1)))
+        parts = [merge(lines[0][tap], lines[1][tap], tap) for tap in range(3)]
+        at = pl.ds(chunk * (ROWS // 2), ROWS // 2)
+        store_pairs(odd, at, ROWS // 2, parts)
+        late = []
+        for tap in range(3):
+            late.append(jnp.concatenate([last[tap][None], parts[tap][0 : ROWS - 1]], axis=0))
+            last[tap] = parts[tap][ROWS - 1]
+        store_pairs(even, at, ROWS // 2, late)
         return 0
 
     lax.fori_loop(0, CHUNKS, run_merge, 0)
+    nothing = jnp.zeros((1, STRIDE, C), F32)
+    ends = [jnp.concatenate([last[tap][None], nothing], axis=0) for tap in range(3)]
+    store_pairs(even, pl.ds(WIN // 2, 1), 1, ends)
 
     for copy in copies_two:
         copy.wait()
     tails(w_two, tail_two)
-    counted = cover[0] + cover[1]
-    counted = jnp.concatenate([counted[0:8] + cover[2, 0:8], counted[8:STRIDE]], axis=0)
-
-    def run_two(chunk):
-        value = convolve(0, chunk, w_two, tail_two).reshape(ROWS, WIN, C)
-        at = pl.ds(chunk * ROWS, ROWS)
+    counted = cover[0, 1] + cover[1, 1]
+    counted = jnp.concatenate([counted[0:8] + wrap[1], counted[8:STRIDE]], axis=0)
+
+    def run_two(pair, count):
+        def flat(source, at, number):
+            return source[at : at + number, :, 0:DEPTH].reshape(number * 2 * STRIDE, DEPTH)
+
+        sources = [flat(even, pair, count), flat(odd, pair, count), flat(even, pair + 1, count)]
+        value = taps(sources, flat(even, pair, count + 1), STRIDE, w_two, tail_two)
+        value = value.reshape(2 * count, STRIDE, C)
+        at = slice(2 * pair, 2 * pair + 2 * count)
         first, second = start[0, at].astype(F32), start[1, at].astype(F32)
-        value = (value + merge(first, second))[:, 0:STRIDE] + counted * vec[7:8, :]
-        band[pl.ds(front + chunk * ROWS, ROWS)] = value
-
-    def run_chunks(chunks):
-        if len(chunks) == 0:
-            return
-        step = chunks[1] - chunks[0]
-
-        def one(index, _):
-            run_two(chunks[0] + index * step)
-            return 0
-
-        lax.fori_loop(0, len(chunks), one, 0)
-
-    run_chunks(plan["first"])
+        value = value + merge(first, second, 1) + counted * line_of(conv_two_bias)
+        band[front + 2 * pair : front + 2 * pair + 2 * count] = value
+
+    for pair, count in plan["first"]:
+        run_two(pair, count)
 
     def stage(target, base, count):
         def one(pair, _):
@@ -448,9 +505,10 @@
         copy.start()
         started.append(copy)
 
-    run_chunks(plan["then"])
+    for pair, count in plan["then"]:
+        run_two(pair, count)
     for copy in started:
-        copy.wait()
+        copy.wait_recv()
 
     scale_cols = 1.0 / counted
 
@@ -481,19 +539,26 @@
 
         lax.fori_loop(low, high, one, 0)
 
+    for copy in lat_copies + started:
+        copy.wait_send()
+
 
 def block_kernel(name, row_axis, ident, operands):
     plan = PLANS[name]
     hbm = pl.BlockSpec(memory_space=pl.ANY)
-    smem = pl.BlockSpec(memory_space=pltpu.SMEM)
     vmem = pl.BlockSpec(memory_space=pltpu.VMEM)
     n_prev, n_next = max(plan["prev"], 2), max(plan["next"], 2)
     ext_rows = 56 if plan["lead"] else 40
     band_rows = plan["front"] + WIN + plan["back"]
     scratch = [
+        pltpu.SMEM((2,), jnp.int32),
+        pltpu.SMEM((1,), jnp.int32),
+        pltpu.VMEM((LATC, STRIDE, STRIDE), BF16),
+        pltpu.VMEM((3, 3, LATC, C), BF16),
         pltpu.VMEM((2, ext_rows, 128), F32),
-        pltpu.VMEM((8, C), F32),
-        pltpu.VMEM((2, TEMB), F32),
+    ]
+    scratch += [pltpu.VMEM((C,), F32)] * 8 + [pltpu.VMEM((TEMB,), F32)] * 2
+    scratch += [
         pltpu.VMEM((C, TEMB), BF16),
         pltpu.VMEM((TEMB, TEMB), BF16),
         pltpu.VMEM((C, TEMB), BF16),
@@ -504,23 +569,28 @@
         pltpu.VMEM((128, C), BF16),
         pltpu.VMEM((2, WIN, MAIN), F32),
         pltpu.VMEM((2, 2, WIN, C), F32),
-        pltpu.VMEM((3, WIN, C), F32),
+        pltpu.VMEM((2, 3, STRIDE, C), F32),
+        pltpu.VMEM((3, 8, C), F32),
         pltpu.VMEM((C, C), BF16),
         pltpu.VMEM((8, C), F32),
         pltpu.VMEM((2, WIN + 2, WIN, 128), F32),
         pltpu.VMEM((2, WIN, WIN, C), BF16),
         pltpu.VMEM((2, WIN + 2, WIN, 4 * MAIN), BF16),
         pltpu.VMEM((2, WIN, WIN, C), F32),
+        pltpu.VMEM((3, STRIDE, C), F32),
+        pltpu.VMEM((WIN // 2 + 1, 2 * STRIDE, 4 * MAIN), BF16),
+        pltpu.VMEM((WIN // 2, 2 * STRIDE, 4 * MAIN), BF16),
         pltpu.VMEM((band_rows, STRIDE, C), F32),
-        pltpu.VMEM((2 * CHUNKS, 8, C), F32),
-        pltpu.VMEM((2 * CHUNKS, 8, C), F32),
+        pltpu.VMEM((2, 8, C), F32),
+        pltpu.VMEM((2, 8, C), F32),
         pltpu.VMEM((2, 2, 8, C), F32),
         pltpu.VMEM((2, 2, 8, C), F32),
         pltpu.VMEM((n_prev // 2, 2 * STRIDE, C), BF16),
         pltpu.VMEM((n_next // 2, 2 * STRIDE, C), BF16),
         pltpu.VMEM((n_next // 2, 2 * STRIDE, C), BF16),
         pltpu.VMEM((n_prev // 2, 2 * STRIDE, C), BF16),
-        pltpu.SemaphoreType.DMA((2,)),
+        pltpu.SemaphoreType.DMA((4,)),
+        pltpu.SemaphoreType.DMA((10,)),
         pltpu.SemaphoreType.DMA((3,)),
         pltpu.SemaphoreType.DMA((2, 18)),
         pltpu.SemaphoreType.DMA((5,)),
@@ -531,7 +601,7 @@
     return pl.pallas_call(
         functools.partial(body, plan, row_axis),
         out_shape=jax.ShapeDtypeStruct((STRIDE, STRIDE, C), F32),
-        in_specs=[smem, smem, vmem, vmem] + [hbm] * 7,
+        in_specs=[hbm] * 19,
         out_specs=vmem,
         scratch_shapes=scratch,
         compiler_params=pltpu.CompilerParams(
@@ -566,33 +636,32 @@
     conv_two_weight,
     conv_two_bias,
 ):
-    vec = jnp.stack(
-        [
-            conv_in_bias,
-            norm_one_gain,
-            norm_one_shift,
-            conv_one_bias,
-            time_proj_bias,
-            norm_two_gain,
-            norm_two_shift,
-            conv_two_bias,
-        ]
-    )
-    tvec = jnp.stack([time_one_bias, time_two_bias])
     operands = (
         offsets,
         timestep,
         latent,
         conv_in_weight,
-        vec,
-        tvec,
+        conv_in_bias,
+        norm_one_gain,
+        norm_one_shift,
+        conv_one_bias,
+        time_proj_bias,
+        norm_two_gain,
+        norm_two_shift,
+        conv_two_bias,
+        time_one_bias,
+        time_two_bias,
         conv_one_weight,
         conv_two_weight,
         time_one_weight,
         time_two_weight,
         time_proj_weight.T,
     )
-    return block_kernel("any", row_axis, 0, operands)
+    branches = [
+        functools.partial(block_kernel, name, row_axis, place)
+        for place, name in enumerate(("low", "mid", "high"))
+    ]
+    return lax.switch(offsets[0] >> 3, branches, operands)
 
 
 def solution(mesh):

time: 54.2 us -> 37.7 us (0.70)
  local copies, waits for them, and re-layouts: 9.62 us -> 0.91 us
  Pallas kernels: 42.9 us -> 35.3 us
  loops' own time: 0 us -> 0.69 us
  other arithmetic: 0.6 us -> 0 us
    pallas_call x1, Pallas kernels: 42.9 us -> 35.3 us  [block_kernel(): pl.pallas_call(functools.partial(body, plan, row_axis), out_shape=jax.Sha...]
    another operation x11 -> x0, local copies, waits for them, and re-layouts: 7.49 us -> none  [the longest x9 6.09 us: on_device(): jnp.stack([conv_in_bias, norm_one_gain, norm_one_shift, conv_one_bias, ti...]
    unnamed x1, local copies, waits for them, and re-layouts: 2.14 us -> 0.91 us
    another operation x0 -> x1, loops' own time: none -> 0.69 us  [on_device(): return lax.switch(offsets[0] >> 3, branches, operands)]
    another operation x1 -> x0, other arithmetic: 0.6 us -> none  [on_device(): tvec = jnp.stack([time_one_bias, time_two_bias])]
where the time goes in v2:
time: 37.7 us; the launch traced here: 37.6 us
  Pallas kernels  35.3 us (94%)
  local copies, waits for them, and re-layouts  0.91 us (2%)
  loops' own time  0.69 us (2%)
  between operations  0.66 us (2%)
    pallas_call x1, Pallas kernels, block_kernel(): pl.pallas_call(functools.partial(body, plan, row_axis), out_shape=jax.Sha...  35.3 us
    unnamed x1, local copies, waits for them, and re-layouts  0.91 us

profile of v2, /device:TPU:16, one launch (start us, length us, event | category | flops | bytes accessed | tf_op | source)
XLA Modules:
  0.0 37.6 jit_solution(12223392294178226622)
XLA Ops:
  0.7 36.0 %conditional.1 = (f32[24,24,320]{2,1,0:T(8,128)S(1)}) conditional(s32[]{:T(128)} %bitcast, (s32[2]{0:T(128)}, s32[1]{0:T(128)}, bf16[4,24,24]{2,1,0:T(8,128)(2,1)}, bf16[3,3,4,320]{3,2,1,0:T(4,128)(2,1)}, f32[320]{0:T(512)}, /*index=5*/f32[320]{0:T(512)}, f32[320]{0:T(512)}, f32[320]{0:T(512)}, f32[320]{0:T(512)}, f32[320]{0:T(512)}, ...), branch_computations={%region_0.0_spmd, %region_1.0_spmd, %region_2.0_spmd} | conditional | flops 5662310400 | bytes 10000008 | solution.py:664
  1.1 35.3 %panorama_block.5 = f32[24,24,320]{2,1,0:T(8,128)S(1)} custom-call(s32[2]{0:T(128)} %get-tuple-element.161.offsets_hbm, s32[1]{0:T(128)} %get-tuple-element.162.timestep_hbm, bf16[4,24,24]{2,1,0:T(8,128)(2,1)} %get-tuple-element.163.latent_hbm, bf16[3,3,4,320]{3,2,1,0:T(4,128)(2,1)} %get-tuple-element.164.conv_in_hbm, ...), custom_call_target="tpu_custom_call" | custom-call | flops 5662310400 | bytes 10000000 | tf_op jit(solution)/shard_map/cond/branch_2_fun/panorama_block/pallas_call | solution.py:601
  36.7 0.9 %copy.27 = f32[24,24,320]{2,1,0:T(8,128)} copy(f32[24,24,320]{2,1,0:T(8,128)S(1)} %get-tuple-element.180) | data formatting | bytes 1474560

commit v3 on v2

--- a/solution.py
+++ b/solution.py
@@ -238,10 +238,6 @@
         )
         copy.start()
         lat_copies.append(copy)
-    for copy in copies_one:
-        copy.start()
-    for copy in copies_two:
-        copy.start()
 
     tap = iota((MAIN, 128), 1)
     from_lane = iota((MAIN, 128), 0)
@@ -294,6 +290,8 @@
 
     for copy in small:
         copy.wait()
+    for copy in copies_one:
+        copy.start()
     freq = jnp.exp(-math.log(10000.0) * iota((8, HALF), 1).astype(F32) / HALF)
     angle = timestep_ref[0].astype(F32) * freq
     cosine = jnp.concatenate([jnp.cos(angle)] * 2, axis=0).astype(BF16)
@@ -310,17 +308,28 @@
 
     for copy in lat_copies:
         copy.wait_recv()
+    for copy in copies_two:
+        copy.start()
 
     lane = iota((1, WIN, 128), 2) >> 2
     lane_row = lane // 3
     lane_col = lane - 3 * lane_row
 
+    def fold(value):
+        return jnp.sum(value.reshape(-1, 8, C), axis=0)
+
     def keep_moments(window, value):
-        mean = jnp.sum(value, axis=0, keepdims=True) * (1.0 / AREA)
-        diff = value - mean
-        means[window] = jnp.broadcast_to(mean, (8, C))
-        spread = jnp.sum(diff * diff, axis=0, keepdims=True) * (1.0 / AREA)
-        spreads[window] = jnp.broadcast_to(spread, (8, C))
+        pivot = value[0:1]
+        once = jnp.zeros((8, C), F32)
+        twice = jnp.zeros((8, C), F32)
+        for at in range(0, AREA, 256):
+            diff = value[at : at + 256] - pivot
+            once = once + fold(diff)
+            twice = twice + fold(diff * diff)
+        once = jnp.sum(once, axis=0, keepdims=True) * (1.0 / AREA)
+        twice = jnp.sum(twice, axis=0, keepdims=True) * (1.0 / AREA)
+        means[window] = jnp.broadcast_to(pivot + once, (8, C))
+        spreads[window] = jnp.broadcast_to(jnp.maximum(twice - once * once, 0.0), (8, C))
 
     def norm_lines(target, gain, offset):
         spare = jnp.zeros((6, C), F32)
@@ -383,13 +392,13 @@
         return half * jnp.tanh(half) + half
 
     def run_act(step, _):
-        window, chunk = step // CHUNKS, lax.rem(step, CHUNKS)
+        window, chunk = step // CHUNKS, step % CHUNKS
         value = start[window, pl.ds(chunk * ROWS, ROWS)].astype(F32)
         value = activate(value, norm_one, window)
         store_act(window, chunk, three_columns(value, window))
         return 0
 
-    lax.fori_loop(0, 2 * CHUNKS, run_act, 0)
+    lax.fori_loop(0, CHUNKS, run_act, 0)
 
     def tails(weights, target):
         blocks = [weights[dy, :, MAIN:C] for dy in range(3)]
@@ -420,7 +429,10 @@
         keep_moments(window, value)
         return 0
 
-    lax.fori_loop(0, 2, run_one, 0)
+    for step in range(CHUNKS, 2 * CHUNKS):
+        run_act(step, 0)
+    run_one(0, 0)
+    run_one(1, 0)
     norm_lines(norm_two, line_of(gain_two), line_of(move_two))
 
     def merge(first, second, tap):
@@ -659,9 +671,9 @@
     )
     branches = [
         functools.partial(block_kernel, name, row_axis, place)
-        for place, name in enumerate(("low", "mid", "high"))
+        for place, name in enumerate(("high", "mid", "low"))
     ]
-    return lax.switch(offsets[0] >> 3, branches, operands)
+    return lax.switch(2 - (offsets[0] >> 3), branches, operands)
 
 
 def solution(mesh):

time: 37.7 us -> 35.4 us (0.939)
  Pallas kernels: 35.3 us -> 33.5 us
  loops' own time: 0.69 us -> 0.24 us
    pallas_call x1, Pallas kernels: 35.3 us -> 33.5 us  [block_kernel(): pl.pallas_call(functools.partial(body, plan, row_axis), out_shape=jax.Sha...]
    another operation x1, loops' own time: 0.69 us -> 0.24 us  [on_device(): return lax.switch(2 - (offsets[0] >> 3), branches, operands)]
where the time goes in v3:
time: 35.4 us; the launch traced here: 35.3 us
  Pallas kernels  33.5 us (95%)
  local copies, waits for them, and re-layouts  0.91 us (3%)
  between operations  0.66 us (2%)
    pallas_call x1, Pallas kernels, block_kernel(): pl.pallas_call(functools.partial(body, plan, row_axis), out_shape=jax.Sha...  33.5 us
    unnamed x1, local copies, waits for them, and re-layouts  0.91 us

profile of v3, /device:TPU:16, one launch (start us, length us, event | category | flops | bytes accessed | tf_op | source)
XLA Modules:
  0.0 35.3 jit_solution(3749695448269919470)
XLA Ops:
  0.7 33.7 %conditional.1 = (f32[24,24,320]{2,1,0:T(8,128)S(1)}) conditional(s32[]{:T(128)} %bitcast, (s32[2]{0:T(128)}, s32[1]{0:T(128)}, bf16[4,24,24]{2,1,0:T(8,128)(2,1)}, bf16[3,3,4,320]{3,2,1,0:T(4,128)(2,1)}, f32[320]{0:T(512)}, /*index=5*/f32[320]{0:T(512)}, f32[320]{0:T(512)}, f32[320]{0:T(512)}, f32[320]{0:T(512)}, f32[320]{0:T(512)}, ...), branch_computations={%region_0.0_spmd, %region_1.0_spmd, %region_2.0_spmd} | conditional | flops 5662310400 | bytes 10000008 | solution.py:676
  0.7 33.5 %panorama_block.3 = f32[24,24,320]{2,1,0:T(8,128)S(1)} custom-call(s32[2]{0:T(128)} %get-tuple-element.122.offsets_hbm, s32[1]{0:T(128)} %get-tuple-element.124.timestep_hbm, bf16[4,24,24]{2,1,0:T(8,128)(2,1)} %get-tuple-element.125.latent_hbm, bf16[3,3,4,320]{3,2,1,0:T(4,128)(2,1)} %get-tuple-element.126.conv_in_hbm, ...), custom_call_target="tpu_custom_call" | custom-call | flops 5662310400 | bytes 10000000 | tf_op jit(solution)/shard_map/cond/branch_0_fun/panorama_block/pallas_call | solution.py:613
  34.4 0.9 %copy.27 = f32[24,24,320]{2,1,0:T(8,128)} copy(f32[24,24,320]{2,1,0:T(8,128)S(1)} %get-tuple-element.180) | data formatting | bytes 1474560
